TPU v7x, 768 devices: a whole 4x8x12 slice. The times are simulated.
768 devices in a mesh: tensor: 32 (over x, y), contract: 24 (over z, core).
Axes of the slice: x: 4, y: 8, z: 12, core: 2. Of those that a mesh axis runs over, the one named last changes fastest.
Arguments:
- amplitudes: bfloat16 [32, 12, 96, 3072], P('tensor', None, None, 'contract'), may hold values from -6 to 6
- pair_mask: int32 [32, 12], P('tensor'), may hold values 0 or 1
- tile_mask: int32 [24], replicated, may hold values 0 or 1
- cycle_integrals: bfloat16 [12, 3072, 12, 128], P(None, 'contract'), may hold values from -0.03125 to 0.03125
- ladder_integrals: bfloat16 [8, 3072, 96, 128], P(None, 'contract', None, 'tensor'), may hold values from -0.0390625 to 0.0390625
Outputs:
- residual: bfloat16 [32, 12, 96, 128], P('tensor', None, 'contract')
All inputs are finite; a program needn't handle non-finite values. No bound on the sum of `pair_mask` on one device may be relied on, other than what follows from the above.
Results may differ from a plain program's by a relative error of at most 0.0013.
Values may be sent and summed in bfloat16 or wider, within the bound.
A program may use at most 64 MiB of HBM per device.

v0:
```python
import jax
import jax.numpy as jnp
from jax import lax
from jax.sharding import PartitionSpec as P


def body(amplitudes, pair_mask, tile_mask, cycle_integrals, ladder_integrals):
    local_rows, occupied, window, tile_edge = amplitudes.shape
    ladder_width = ladder_integrals.shape[0]
    local_cols = ladder_integrals.shape[3]
    masked = amplitudes * pair_mask[:, :, None, None].astype(jnp.bfloat16)
    section = lax.axis_index("contract")
    kept_tile = lax.dynamic_index_in_dim(tile_mask, section, 0, keepdims=False).astype(jnp.bfloat16)
    ladder_right = (ladder_integrals * kept_tile).reshape(
        ladder_width * tile_edge, window * local_cols
    )
    ladder_left = masked[:, :, :ladder_width, :]
    piece = lax.all_gather(ladder_left, "tensor", axis=0, tiled=True)
    row_count = piece.shape[0]
    product = jnp.dot(
        piece.reshape(row_count * occupied, ladder_width * tile_edge),
        ladder_right,
        preferred_element_type=jnp.float32,
    )
    ladder_term = product.reshape(row_count, occupied, window, local_cols)
    cycle_left = jnp.transpose(masked, (0, 2, 1, 3)).reshape(
        local_rows * window, occupied * tile_edge
    )
    cycle_right = cycle_integrals.reshape(occupied * tile_edge, -1)
    cycle_term = jnp.dot(cycle_left, cycle_right, preferred_element_type=jnp.float32)
    cycle_term = jnp.transpose(cycle_term.reshape(local_rows, window, occupied, -1), (0, 2, 1, 3))
    ladder_sum, cycle_sum = (
        lax.psum_scatter(ladder_term, "contract", scatter_dimension=2, tiled=True),
        lax.psum_scatter(cycle_term, "contract", scatter_dimension=2, tiled=True),
    )
    summed = (
        lax.all_to_all(ladder_sum, "tensor", split_axis=0, concat_axis=3, tiled=True) + cycle_sum
    )
    return summed.astype(jnp.bfloat16)


def solution(mesh):
    in_specs = (
        P("tensor", None, None, "contract"),
        P("tensor", None),
        P(),
        P(None, "contract", None, None),
        P(None, "contract", None, "tensor"),
    )
    out_specs = P("tensor", None, "contract", None)
    return jax.shard_map(body, mesh=mesh, in_specs=in_specs, out_specs=out_specs, check_vma=False)
```

profile of v0, /device:TPU:1, one launch (start us, length us, event | category | flops | bytes accessed | tf_op | source)
XLA Modules:
  0.0 294.7 jit_solution(2679086965600183719)
XLA Ops:
  6.5 0.7 convert_bitcast_fusion
  7.2 1.0 broadcast_multiply_fusion.1
  8.2 1.1 fusion.7
  9.3 1.2 dynamic_slice.4
  11.2 1.2 broadcast_multiply_fusion
  12.4 0.9 copy.44
  13.5 0.3 dot_general.20
  13.8 39.5 %all_gather.3 = bf16[32,12,8,128]{3,2,1,0:T(8,128)(2,1)S(1)} all-gather(bf16[1,12,8,128]{3,2,1,0:T(8,128)(2,1)S(1)} %slice.4), channel_id=1, replica_groups=mesh['tensor'=32,'contract'=24] {'tensor'}, dimensions={0}, use_global_device_ids=true | all-gather | bytes 811008 | tf_op jit(solution)/shard_map/all_gather | solution.py:18
  53.5 0.3 reshape.35
  54.2 6.0 %copy.49 = bf16[12,128,12,128]{3,2,1,0:T(8,128)(2,1)S(1)} copy(bf16[12,128,12,128]{3,1,2,0:T(8,128)(2,1)} %param.8) | data formatting | bytes 9437184 | tf_op args[3]
  60.2 4.6 %copy.65 = bf16[192,8,12,128]{3,1,2,0:T(8,128)(2,1)} copy(bf16[192,8,12,128]{3,2,1,0:T(8,128)(2,1)S(1)} %bitcast.55) | data formatting | bytes 9437184
  64.8 6.6 %copy.50 = bf16[1536,1536]{1,0:T(8,128)(2,1)} copy(bf16[1536,1536]{0,1:T(8,128)(2,1)} %bitcast.57) | data formatting | bytes 9437184 | tf_op jit(solution)/shard_map/dot_general | solution.py:30
  71.4 2.8 fusion
  74.3 2.4 convolution_bitcast_fusion
  76.7 1.3 dynamic-slice
  78.6 186.7 %all-reduce.5.cloned.1.call-done = (f32[32,12,96,4]{0,2,3,1:T(8,128)}, f32[1,12,96,128]{3,2,1,0:T(8,128)}) async-done(((f32[32,12,96,4]{0,2,3,1:T(8,128)}, f32[1,12,96,128]{3,2,1,0:T(8,128)}), (f32[32,12,96,4]{0,2,3,1:T(8,128)}, f32[1,12,96,128]{3,2,1,0:T(8,128)})) %all-reduce.5.cloned.1.call-update) | async-done | bytes 1179664
  265.3 0.9 constant_dynamic-slice_fusion
  266.2 0.2 copy.46
  266.5 0.3 reshape.46
  266.8 17.8 %all_to_all.18 = f32[32,1,192]{2,1,0:T(1,128)S(1)} all-to-all(f32[32,1,192]{2,1,0:T(1,128)S(1)} %reshape.46), channel_id=1, replica_groups=mesh['tensor'=32,'contract'=24] {'tensor'}, dimensions={0} | all-to-all | bytes 49152 | tf_op jit(solution)/shard_map/all_to_all | solution.py:37
  284.6 0.5 broadcast.1
  285.1 0.7 reduce
  285.8 0.3 reshape.47
  286.4 1.4 fusion.4
  (12 shorter events, 0.9 us)
Async XLA Ops:
  6.5 258.7 %all-reduce.5.cloned.1.call-start = ((), (), s32[]{:S(2)}) async-start(), calls=%async_computation.1 | async-start | bytes 5898240
  71.4 2.8 copy-start
Sparse Core Ops, SparseCore 0:
  76.8 188.4 all-reduce.4
where the time goes:
time: 298 us; the launch traced here: 295 us
  waiting for transfers between devices  187 us (63%)
  blocking collectives  57.3 us (19%)
  local copies, waits for them, and re-layouts  24.5 us (8%)
  between operations  14.9 us (5%)
  other arithmetic  6.08 us (2%)
  matrix products  5.21 us (2%)
    unnamed x2, waiting for transfers between devices  187 us
    all_gather x1, blocking collectives, body(): piece = lax.all_gather(ladder_left, 'tensor', axis=0, tiled=True)  39.5 us
    all_to_all x1, blocking collectives, body(): lax.all_to_all(ladder_sum, 'tensor', split_axis=0, concat_axis=3, tiled=T...  17.8 us
    unnamed x9, local copies, waits for them, and re-layouts  13.6 us
    dot_general x1, local copies, waits for them, and re-layouts, body(): jnp.dot(cycle_left, cycle_right, preferred_element_type=jnp.float32)  6.64 us
  transfers between devices with their start and end apart: 1, of which 1 were waited for; matrix products, arithmetic and copies ran while one was open for 0% of the time, Pallas kernels for 0%

commit v1 on v0

v1 whole, which is shorter than its diff:
```python
import jax
import jax.numpy as jnp
from jax import lax
from jax.experimental import pallas as pl
from jax.experimental.pallas import tpu as pltpu
from jax.sharding import PartitionSpec as P

X, Y, Z = 4, 8, 12
PLANE = X * Y
J, WIN, TILE, CW, AB = 12, 96, 128, 8, 384
MESH = pl.DeviceIdType.MESH
F32, BF16 = jnp.float32, jnp.bfloat16
Y_FAR = (4, 3, 5, 2, 6, 1, 7)
Y_NEAR = Y_FAR[::-1]
X_FAR = (2, 1, 3)
Z_FAR = (6, 5, 7, 4, 8, 3, 9, 2, 10, 1, 11)


def kernel(
    pm, tm, a_hbm, w_hbm, g_hbm, out,
    av, am, wv, gv, ag, mf, rhs, pc, rc, zc, pz, rz, zr, r1, w2, w3, zz,
    load_sem, w_sem, ag_s, ag_r, x_s, x_r, zc_s, zc_r, zl_s, zl_r, a2a_s, a2a_r, self_sem,
):
    t = lax.axis_index("tensor")
    s = lax.axis_index("contract")
    x, y, z, c = t // Y, t % Y, s // 2, s % 2

    def plane(dx, dy):
        return {"tensor": lax.rem(x + dx + X, X) * Y + lax.rem(y + dy + Y, Y), "contract": s}

    def column(dz):
        return {"tensor": t, "contract": lax.rem(z + dz + Z, Z) * 2 + c}

    sibling = {"tensor": t, "contract": z * 2 + 1 - c}

    def remote(src, dst, ss, rs, to):
        return pltpu.make_async_remote_copy(
            src_ref=src, dst_ref=dst, send_sem=ss, recv_sem=rs, device_id=to, device_id_type=MESH
        )

    load_a = pltpu.make_async_copy(a_hbm, av, load_sem.at[0])
    load_a.start()
    barrier = pltpu.get_barrier_semaphore()
    others = [(dx, dy) for dx in range(X) for dy in range(Y) if (dx, dy) != (0, 0)]
    for dx, dy in others:
        pl.semaphore_signal(barrier, inc=1, device_id=plane(dx, dy), device_id_type=MESH)
    for dz in Z_FAR:
        pl.semaphore_signal(barrier, inc=1, device_id=column(dz), device_id_type=MESH)
    pl.semaphore_signal(barrier, inc=1, device_id=sibling, device_id_type=MESH)
    load_w = [
        pltpu.make_async_copy(w_hbm.at[:, 2 * q : 2 * q + 2], wv.at[:, 2 * q : 2 * q + 2], w_sem.at[q])
        for q in range(J // 2)
    ]
    for copy in load_w:
        copy.start()
    load_g = [
        pltpu.make_async_copy(g_hbm.at[k], gv.at[:, k * TILE : (k + 1) * TILE], load_sem.at[1 + k])
        for k in range(CW)
    ]
    for copy in load_g:
        copy.start()

    load_a.wait()
    kept = tm[0, s].astype(F32)
    for j in range(J):
        m = pm[0, j].astype(F32)
        ag[0, j * CW : (j + 1) * CW, :] = (av[j, :CW, :].astype(F32) * (m * kept)).astype(BF16)
    pl.semaphore_wait(barrier, len(others) + len(Z_FAR) + 1)

    def gather(dy, dx, src, to):
        slot = dy * X + dx
        return remote(src, ag.at[slot], ag_s.at[slot], ag_r.at[slot], to)

    gathers = []
    for dy in Y_FAR:
        gathers.append(gather(dy, 0, ag.at[0], plane(0, -dy)))
    for dx in X_FAR:
        gathers.append(gather(0, dx, ag.at[0], plane(-dx, 0)))
    for copy in gathers:
        copy.start()

    def place(slot):
        il = slot
        block = ag[slot].astype(F32)
        for j in range(J):
            mf[pl.ds(j * PLANE + il, CW, stride=AB), :] = block[j * CW : (j + 1) * CW, :]

    for j in range(J):
        m = pm[0, j].astype(F32)
        am[:, j * TILE : (j + 1) * TILE] = (av[j].astype(F32) * m).astype(BF16)
    left = am[...]
    for q in range(J // 2):
        load_w[q].wait()
        right = jnp.concatenate(
            [wv[:, 2 * q + h].reshape(J * TILE, TILE) for h in range(2)], axis=1
        )
        product = jnp.dot(left, right, preferred_element_type=F32)
        for zd in range(Z):
            for cd in range(2):
                rows = product[zd * 8 + cd * 4 : zd * 8 + cd * 4 + 4, :]
                pc[cd, zd, 8 * q : 8 * q + 8, :] = jnp.concatenate([rows[:, :TILE], rows[:, TILE:]], axis=0)
    cycle_swap = remote(pc.at[1 - c], rc, x_s.at[0], x_r.at[0], sibling)
    cycle_swap.start()

    for dy in Y_NEAR:
        gather(dy, 0, ag.at[0], plane(0, -dy)).wait_recv()
        for dx in X_FAR:
            copy = gather(dy, dx, ag.at[dy * X], plane(-dx, 0))
            copy.start()
            gathers.append(copy)

    cycle_swap.wait()
    cycle_sends = []
    rc[...] = rc[...] + pc[c]
    for dz in Z_FAR:
        copy = remote(rc.at[lax.rem(z + Z - dz, Z)], zc.at[dz - 1], zc_s.at[dz - 1], zc_r.at[dz - 1], column(-dz))
        copy.start()
        cycle_sends.append(copy)

    place(0)
    for dy in Y_NEAR:
        place(dy * X)
    for dy in (0,) + Y_NEAR:
        for dx in (1, 3, 2):
            gather(dy, dx, ag.at[0], plane(-dx, 0)).wait_recv()
            place(dy * X + dx)
    for k in range(CW):
        rhs[:, k * TILE : (k + 1) * TILE] = mf[k * AB : (k + 1) * AB, :].astype(BF16)
    for copy in load_g:
        copy.wait()
    ladder = lax.dot_general(gv[...], rhs[...], (((1,), (1,)), ((), ())), preferred_element_type=F32)
    for zd in range(Z):
        for cd in range(2):
            row = zd * 32 + cd * 16
            pz[cd, zd] = ladder[row : row + 16, :]
    ladder_swap = remote(pz.at[1 - c], rz, x_s.at[1], x_r.at[1], sibling)
    ladder_swap.start()
    ladder_swap.wait()
    rz[...] = rz[...] + pz[c]
    ladder_sends = []
    for dz in Z_FAR:
        copy = remote(rz.at[lax.rem(z + Z - dz, Z)], zr.at[dz - 1], zl_s.at[dz - 1], zl_r.at[dz - 1], column(-dz))
        copy.start()
        ladder_sends.append(copy)

    cycle = rc[z]
    for dz in range(1, Z):
        remote(rc.at[0], zc.at[dz - 1], zc_s.at[dz - 1], zc_r.at[dz - 1], column(-dz)).wait_recv()
        cycle = cycle + zc[dz - 1]

    total = rz[z]
    for dz in (1, 11, 2, 10, 3, 9, 4, 8, 5, 7, 6):
        remote(rz.at[0], zr.at[dz - 1], zl_s.at[dz - 1], zl_r.at[dz - 1], column(-dz)).wait_recv()
        total = total + zr[dz - 1]
    for k in range(3):
        r1[16 * k : 16 * k + 16, :] = total[:, k * TILE : (k + 1) * TILE]
    flipped = jnp.concatenate(
        [
            jnp.transpose(jnp.concatenate([r1[pl.ds(16 * k + b, 4, stride=4), :] for b in range(4)], axis=0))
            for k in range(3)
        ],
        axis=0,
    )
    lane = lax.broadcasted_iota(jnp.int32, (PLANE, TILE), 1)
    pieces = [jnp.zeros((PLANE, TILE), F32) for _ in range(4)]
    for j in range(J):
        block = jnp.concatenate(
            [flipped[j * PLANE : (j + 1) * PLANE, :], jnp.zeros((PLANE, TILE - 16), F32)], axis=1
        )
        block = pltpu.roll(block, 4 * j, 1)
        for b in range(4):
            low = 4 * (j + b)
            pieces[b] = jnp.where((lane >= low) & (lane < low + 4), block, pieces[b])
    for b in range(4):
        piece = pieces[b] if b == 0 else pltpu.roll(pieces[b], TILE - 4 * b, 1)
        w2[pl.ds(b, PLANE, stride=4), :] = piece
    w3[...] = w2[...].reshape(PLANE, 4, TILE)
    own = pltpu.make_async_copy(w3.at[0], zz.at[t], self_sem)
    own.start()
    blocks = []
    for dx, dy in sorted(others, key=lambda o: -min(o[0], X - o[0]) - min(o[1], Y - o[1])):
        slot = dy * X + dx
        copy = remote(w3.at[slot], zz.at[t], a2a_s.at[slot], a2a_r.at[t], plane(dx, dy))
        copy.start()
        blocks.append(copy)
    own.wait()
    for dx, dy in others:
        src = plane(dx, dy)["tensor"]
        remote(w3.at[0], zz.at[src], a2a_s.at[0], a2a_r.at[src], plane(dx, dy)).wait_recv()
    final = jnp.transpose(zz[...].reshape(PLANE * 4, TILE))
    out[...] = (final[: J * 4, :] + cycle).astype(BF16)
    for copy in gathers + cycle_sends + ladder_sends + blocks:
        copy.wait_send()


def body(amplitudes, pair_mask, tile_mask, cycle_integrals, ladder_integrals):
    w = jnp.transpose(cycle_integrals, (0, 2, 1, 3))
    g = jnp.transpose(ladder_integrals, (0, 2, 3, 1)).reshape(CW, AB, TILE)
    smem = pl.BlockSpec(memory_space=pltpu.SMEM)
    anywhere = pl.BlockSpec(memory_space=pl.ANY)
    dma = pltpu.SemaphoreType.DMA
    out = pl.pallas_call(
        kernel,
        out_shape=jax.ShapeDtypeStruct((J * 4, TILE), BF16),
        in_specs=[smem, smem, anywhere, anywhere, anywhere],
        out_specs=pl.BlockSpec(memory_space=pltpu.VMEM),
        scratch_shapes=[
            pltpu.VMEM((J, WIN, TILE), BF16),
            pltpu.VMEM((WIN, J * TILE), BF16),
            pltpu.VMEM((J, J, TILE, TILE), BF16),
            pltpu.VMEM((AB, CW * TILE), BF16),
            pltpu.VMEM((PLANE, J * CW, TILE), BF16),
            pltpu.VMEM((CW * AB, TILE), F32),
            pltpu.VMEM((AB, CW * TILE), BF16),
            pltpu.VMEM((2, Z, J * 4, TILE), F32),
            pltpu.VMEM((Z, J * 4, TILE), F32),
            pltpu.VMEM((Z - 1, J * 4, TILE), F32),
            pltpu.VMEM((2, Z, 16, AB), F32),
            pltpu.VMEM((Z, 16, AB), F32),
            pltpu.VMEM((Z - 1, 16, AB), F32),
            pltpu.VMEM((48, TILE), F32),
            pltpu.VMEM((PLANE * 4, TILE), F32),
            pltpu.VMEM((PLANE, 4, TILE), F32),
            pltpu.VMEM((PLANE, 4, TILE), F32),
            dma((1 + CW,)), dma((J // 2,)), dma((PLANE,)), dma((PLANE,)), dma((2,)), dma((2,)),
            dma((Z - 1,)), dma((Z - 1,)), dma((Z - 1,)), dma((Z - 1,)), dma((PLANE,)), dma((PLANE,)),
            dma,
        ],
        compiler_params=pltpu.CompilerParams(
            collective_id=0, has_side_effects=True, vmem_limit_bytes=60 * 2**20
        ),
    )(pair_mask, tile_mask.reshape(1, -1), amplitudes[0], w, g)
    return out.reshape(1, J, 4, TILE)


def solution(mesh):
    in_specs = (
        P("tensor", None, None, "contract"),
        P("tensor", None),
        P(),
        P(None, "contract", None, None),
        P(None, "contract", None, "tensor"),
    )
    out_specs = P("tensor", None, "contract", None)
    return jax.shard_map(body, mesh=mesh, in_specs=in_specs, out_specs=out_specs, check_vma=False)
```

time: 298 us -> 59.3 us (0.20); the launches traced: 295 us -> 59.1 us
  waiting for transfers between devices: 187 us -> 0 us
  Pallas kernels: 0 us -> 57.8 us
  blocking collectives: 57.3 us -> 0 us
  local copies, waits for them, and re-layouts: 24.5 us -> 1.31 us
  between operations: 14.9 us -> 0.01 us
  other arithmetic: 6.08 us -> 0 us
  matrix products: 5.21 us -> 0 us
    unnamed x2 -> x0, waiting for transfers between devices: 187 us -> none
    pallas_call x0 -> x1, Pallas kernels: none -> 57.8 us  [body(): pl.pallas_call(kernel, out_shape=jax.ShapeDtypeStruct((J * 4, TILE), BF16...]
    all_gather x1 -> x0, blocking collectives: 39.5 us -> none  [body(): piece = lax.all_gather(ladder_left, 'tensor', axis=0, tiled=True)]
    all_to_all x1 -> x0, blocking collectives: 17.8 us -> none  [body(): lax.all_to_all(ladder_sum, 'tensor', split_axis=0, concat_axis=3, tiled=T...]
    unnamed x9 -> x1, local copies, waits for them, and re-layouts: 13.6 us -> 1.31 us
    dot_general x3 -> x0, local copies, waits for them, and re-layouts: 7.26 us -> none  [the longest x1 6.64 us: body(): jnp.dot(cycle_left, cycle_right, preferred_element_type=jnp.float32)]
    dot_general x2 -> x0, matrix products: 5.21 us -> none  [the longest x1 2.84 us: body(): jnp.dot(piece.reshape(row_count * occupied, ladder_width * tile_edge), la...]
  transfers between devices with their start and end apart: 1 -> 0, of which waited for: 1 -> 0; matrix products, arithmetic and copies ran while one was open for 0% -> 0% of each run, Pallas kernels for 0% -> 0%
where the time goes in v1:
time: 59.3 us; the launch traced here: 59.1 us
  Pallas kernels  57.8 us (97%)
  local copies, waits for them, and re-layouts  1.31 us (2%)
    pallas_call x1, Pallas kernels, body(): pl.pallas_call(kernel, out_shape=jax.ShapeDtypeStruct((J * 4, TILE), BF16...  57.8 us
    unnamed x1, local copies, waits for them, and re-layouts  1.31 us

profile of v1, /device:TPU:1, one launch (start us, length us, event | category | flops | bytes accessed | tf_op | source)
XLA Modules:
  0.0 59.1 jit_solution(806936997316333570)
XLA Ops:
  0.0 57.8 %shard_map.55 = bf16[48,128]{1,0:T(8,128)(2,1)} custom-call(s32[1,12]{1,0:T(1,128)} %pm.1, s32[1,24]{1,0:T(1,128)} %bitcast.11, bf16[12,96,128]{2,1,0:T(8,128)(2,1)} %bitcast.9, bf16[12,12,128,128]{3,2,1,0:T(8,128)(2,1)} %bitcast.7, bf16[8,384,128]{2,1,0:T(8,128)(2,1)} %bitcast.8), custom_call_target="tpu_custom_call" | custom-call | tf_op jit(solution)/shard_map/pallas_call | solution.py:202
  57.8 1.3 %copy.7 = bf16[1,12,4,128]{3,2,1,0:T(4,128)(2,1)} copy(bf16[1,12,4,128]{3,2,1,0:T(4,128)(2,1)} %bitcast.10) | data formatting | bytes 24576

commit v2 on v1

v2 whole, which is shorter than its diff:
```python
import jax
import jax.numpy as jnp
from jax import lax
from jax.experimental import pallas as pl
from jax.experimental.pallas import tpu as pltpu
from jax.sharding import PartitionSpec as P

X, Y, Z = 4, 8, 12
PLANE = X * Y
J, WIN, TILE, CW, AB = 12, 96, 128, 8, 384
MESH = pl.DeviceIdType.MESH
F32, BF16 = jnp.float32, jnp.bfloat16
Y_FAR = (4, 3, 5, 2, 6, 1, 7)
X_FAR = (2, 1, 3)
GI = 16
GC = J * GI
GROUPS = tuple(
    tuple((dy, dx) for dy in rows for dx in (0, 1, 3, 2)) for rows in ((0, 1, 7, 2), (6, 3, 5, 4))
)
Z_FAR = (6, 5, 7, 4, 8, 3, 9, 2, 10, 1, 11)


def hops(slot):
    dy, dx = slot
    return min(dy, Y - dy) + min(dx, X - dx)


def kernel(
    pm, tm, a_hbm, w_hbm, g_hbm, out,
    av, am, wv, gv, ag, mf, rhs, pc, rc, zc, pz, rz, zr, r1, w2, w3, zz,
    load_sem, w_sem, ag_s, ag_r, x_s, x_r, zc_s, zc_r, zl_s, zl_r, a2a_s, a2a_r, self_sem,
):
    t = lax.axis_index("tensor")
    s = lax.axis_index("contract")
    x, y, z, c = t // Y, t % Y, s // 2, s % 2

    def plane(dx, dy):
        return {"tensor": lax.rem(x + dx + X, X) * Y + lax.rem(y + dy + Y, Y), "contract": s}

    def column(dz):
        return {"tensor": t, "contract": lax.rem(z + dz + Z, Z) * 2 + c}

    sibling = {"tensor": t, "contract": z * 2 + 1 - c}

    def remote(src, dst, ss, rs, to):
        return pltpu.make_async_remote_copy(
            src_ref=src, dst_ref=dst, send_sem=ss, recv_sem=rs, device_id=to, device_id_type=MESH
        )

    barrier = pltpu.get_barrier_semaphore()
    others = [(dx, dy) for dx in range(X) for dy in range(Y) if (dx, dy) != (0, 0)]
    line = [plane(dx, dy) for dx, dy in others if 0 in (dx, dy)]
    line += [column(dz) for dz in Z_FAR] + [sibling]
    for peer in line:
        pl.semaphore_signal(barrier, inc=1, device_id=peer, device_id_type=MESH)
    load_a = pltpu.make_async_copy(a_hbm, av, load_sem.at[0])
    load_a.start()
    load_w = [
        pltpu.make_async_copy(w_hbm.at[:, 2 * q : 2 * q + 2], wv.at[:, 2 * q : 2 * q + 2], w_sem.at[q])
        for q in range(J // 2)
    ]
    for copy in load_w:
        copy.start()
    load_g = [
        pltpu.make_async_copy(g_hbm.at[k], gv.at[:, k * TILE : (k + 1) * TILE], load_sem.at[1 + k])
        for k in range(CW)
    ]
    for copy in load_g:
        copy.start()

    load_a.wait()
    kept = tm[0, s].astype(F32)
    for j in range(J):
        m = pm[0, j].astype(F32)
        ag[0, j * CW : (j + 1) * CW, :] = (av[j, :CW, :].astype(F32) * (m * kept)).astype(BF16)
    pl.semaphore_wait(barrier, len(line))

    def gather(dy, dx, src, to):
        slot = dy * X + dx
        return remote(src, ag.at[slot], ag_s.at[slot], ag_r.at[slot], to)

    gathers = []
    for dy in Y_FAR:
        gathers.append(gather(dy, 0, ag.at[0], plane(0, -dy)))
    for dx in X_FAR:
        gathers.append(gather(0, dx, ag.at[0], plane(-dx, 0)))
    for copy in gathers:
        copy.start()

    def place(group, il):
        dy, dx = GROUPS[group][il]
        block = ag[dy * X + dx].astype(F32)
        for j in range(J):
            mf[group, pl.ds(j * GI + il, CW, stride=GC), :] = block[j * CW : (j + 1) * CW, :]

    for j in range(J):
        m = pm[0, j].astype(F32)
        am[:, j * TILE : (j + 1) * TILE] = (av[j].astype(F32) * m).astype(BF16)
    left = am[...]
    for q in range(J // 2):
        load_w[q].wait()
        right = jnp.concatenate(
            [wv[:, 2 * q + h].reshape(J * TILE, TILE) for h in range(2)], axis=1
        )
        product = jnp.dot(left, right, preferred_element_type=F32)
        for zd in range(Z):
            for cd in range(2):
                rows = product[zd * 8 + cd * 4 : zd * 8 + cd * 4 + 4, :]
                pc[cd, zd, 8 * q : 8 * q + 8, :] = jnp.concatenate([rows[:, :TILE], rows[:, TILE:]], axis=0)
    cycle_swap = remote(pc.at[1 - c], rc, x_s.at[0], x_r.at[0], sibling)
    cycle_swap.start()

    for dx in (1, 3, 2):
        gather(0, dx, ag.at[0], plane(-dx, 0)).wait_recv()
        for dy in (1, 7):
            copy = gather(dy, dx, ag.at[dx], plane(0, -dy))
            copy.start()
            gathers.append(copy)
    for dy in (2, 6, 3, 5, 4):
        gather(dy, 0, ag.at[0], plane(0, -dy)).wait_recv()
        for dx in X_FAR:
            copy = gather(dy, dx, ag.at[dy * X], plane(-dx, 0))
            copy.start()
            gathers.append(copy)
    for dy in (1, 7):
        gather(dy, 0, ag.at[0], plane(0, -dy)).wait_recv()

    cycle_swap.wait()
    cycle_sends = []
    rc[...] = rc[...] + pc[c]
    for dz in Z_FAR:
        copy = remote(rc.at[lax.rem(z + Z - dz, Z)], zc.at[dz - 1], zc_s.at[dz - 1], zc_r.at[dz - 1], column(-dz))
        copy.start()
        cycle_sends.append(copy)

    for copy in load_g:
        copy.wait()
    swaps, ladder_sends = [], []

    def pick(group, ils):
        for il in ils:
            dy, dx = GROUPS[group][il]
            if dx:
                if dy:
                    gather(dy, dx, ag.at[0], plane(-dx, 0)).wait_recv()
            place(group, il)

    def multiply(group):
        for k in range(CW):
            rhs[group, :, k * TILE : (k + 1) * TILE] = mf[group, k * GC : (k + 1) * GC, :].astype(BF16)
        ladder = lax.dot_general(
            gv[...], rhs[group], (((1,), (1,)), ((), ())), preferred_element_type=F32
        )
        for zd in range(Z):
            for cd in range(2):
                rows = ladder[zd * 32 + cd * 16 : zd * 32 + cd * 16 + 16, :]
                pz[group, cd, zd, :16, :] = rows[:, :TILE]
                pz[group, cd, zd, 16:, :] = jnp.concatenate([rows[:8, TILE:], rows[8:, TILE:]], axis=1)
        swap = remote(pz.at[group, 1 - c], rz.at[group], x_s.at[1 + group], x_r.at[1 + group], sibling)
        swap.start()
        swaps.append(swap)

    def scatter(group):
        swaps[group].wait()
        rz[group] = rz[group] + pz[group, c]
        for dz in Z_FAR:
            copy = remote(
                rz.at[group, lax.rem(z + Z - dz, Z)], zr.at[group, dz - 1],
                zl_s.at[group, dz - 1], zl_r.at[group, dz - 1], column(-dz),
            )
            copy.start()
            ladder_sends.append(copy)

    pick(0, range(GI))
    multiply(0)
    pick(1, range(4))
    scatter(0)
    pick(1, range(4, GI))
    multiply(1)
    for copy in gathers:
        copy.wait_send()
    scatter(1)

    cycle = rc[z]
    for dz in range(1, Z):
        remote(rc.at[0], zc.at[dz - 1], zc_s.at[dz - 1], zc_r.at[dz - 1], column(-dz)).wait_recv()
        cycle = cycle + zc[dz - 1]
    for copy in cycle_sends:
        copy.wait_send()

    lane = lax.broadcasted_iota(jnp.int32, (GI, TILE), 1)
    blocks = []
    for group in range(2):
        total = rz[group, z]
        for dz in (1, 11, 2, 10, 3, 9, 4, 8, 5, 7, 6):
            remote(
                rz.at[group, 0], zr.at[group, dz - 1], zl_s.at[group, dz - 1], zl_r.at[group, dz - 1], column(-dz)
            ).wait_recv()
            total = total + zr[group, dz - 1]
        r1[:24, :] = total
        r1[24:, :] = pltpu.roll(total[16:, :], 64, 1)
        flipped = jnp.concatenate(
            [
                jnp.transpose(jnp.concatenate([r1[pl.ds(16 * k + b, 4, stride=4), :] for b in range(4)], axis=0))
                for k in range(2)
            ],
            axis=0,
        )
        pieces = [jnp.zeros((GI, TILE), F32) for _ in range(4)]
        for j in range(J):
            block = jnp.concatenate(
                [flipped[j * GI : (j + 1) * GI, :], jnp.zeros((GI, TILE - 16), F32)], axis=1
            )
            block = pltpu.roll(block, 4 * j, 1)
            for b in range(4):
                low = 4 * (j + b)
                pieces[b] = jnp.where((lane >= low) & (lane < low + 4), block, pieces[b])
        for b in range(4):
            piece = pieces[b] if b == 0 else pltpu.roll(pieces[b], TILE - 4 * b, 1)
            w2[pl.ds(b, GI, stride=4), :] = piece
        w3[group] = w2[...].reshape(GI, 4, TILE)
        for il in sorted(range(GI), key=lambda il: -hops(GROUPS[group][il])):
            dy, dx = GROUPS[group][il]
            if (dy, dx) == (0, 0):
                own = pltpu.make_async_copy(w3.at[group, il], zz.at[t], self_sem)
                own.start()
                own.wait()
                continue
            slot = dy * X + dx
            copy = remote(w3.at[group, il], zz.at[t], a2a_s.at[slot], a2a_r.at[t], plane(dx, dy))
            copy.start()
            blocks.append(copy)
    for copy in ladder_sends:
        copy.wait_send()
    for dx, dy in others:
        src = plane(dx, dy)["tensor"]
        remote(w3.at[0, 0], zz.at[src], a2a_s.at[0], a2a_r.at[src], plane(dx, dy)).wait_recv()
    final = jnp.transpose(zz[...].reshape(PLANE * 4, TILE))
    out[...] = (final[: J * 4, :] + cycle).astype(BF16)
    for copy in blocks:
        copy.wait_send()


def body(amplitudes, pair_mask, tile_mask, cycle_integrals, ladder_integrals):
    w = jnp.transpose(cycle_integrals, (0, 2, 1, 3))
    g = jnp.transpose(ladder_integrals, (0, 2, 3, 1)).reshape(CW, AB, TILE)
    smem = pl.BlockSpec(memory_space=pltpu.SMEM)
    anywhere = pl.BlockSpec(memory_space=pl.ANY)
    dma = pltpu.SemaphoreType.DMA
    out = pl.pallas_call(
        kernel,
        out_shape=jax.ShapeDtypeStruct((J * 4, TILE), BF16),
        in_specs=[smem, smem, anywhere, anywhere, anywhere],
        out_specs=pl.BlockSpec(memory_space=pltpu.VMEM),
        scratch_shapes=[
            pltpu.VMEM((J, WIN, TILE), BF16),
            pltpu.VMEM((WIN, J * TILE), BF16),
            pltpu.VMEM((J, J, TILE, TILE), BF16),
            pltpu.VMEM((AB, CW * TILE), BF16),
            pltpu.VMEM((PLANE, J * CW, TILE), BF16),
            pltpu.VMEM((2, CW * GC, TILE), F32),
            pltpu.VMEM((2, GC, CW * TILE), BF16),
            pltpu.VMEM((2, Z, J * 4, TILE), F32),
            pltpu.VMEM((Z, J * 4, TILE), F32),
            pltpu.VMEM((Z - 1, J * 4, TILE), F32),
            pltpu.VMEM((2, 2, Z, 24, TILE), F32),
            pltpu.VMEM((2, Z, 24, TILE), F32),
            pltpu.VMEM((2, Z - 1, 24, TILE), F32),
            pltpu.VMEM((32, TILE), F32),
            pltpu.VMEM((GI * 4, TILE), F32),
            pltpu.VMEM((2, GI, 4, TILE), F32),
            pltpu.VMEM((PLANE, 4, TILE), F32),
            dma((1 + CW,)), dma((J // 2,)), dma((PLANE,)), dma((PLANE,)), dma((3,)), dma((3,)),
            dma((Z - 1,)), dma((Z - 1,)), dma((2, Z - 1)), dma((2, Z - 1)), dma((PLANE,)), dma((PLANE,)),
            dma,
        ],
        compiler_params=pltpu.CompilerParams(
            collective_id=0, has_side_effects=True, vmem_limit_bytes=60 * 2**20
        ),
    )(pair_mask, tile_mask.reshape(1, -1), amplitudes[0], w, g)
    return out.reshape(1, J, 4, TILE)


def solution(mesh):
    in_specs = (
        P("tensor", None, None, "contract"),
        P("tensor", None),
        P(),
        P(None, "contract", None, None),
        P(None, "contract", None, "tensor"),
    )
    out_specs = P("tensor", None, "contract", None)
    return jax.shard_map(body, mesh=mesh, in_specs=in_specs, out_specs=out_specs, check_vma=False)
```

time: 59.3 us -> 57.3 us (0.966)
  the two profiles are of different devices: /device:TPU:1 before, /device:TPU:8 now
where the time goes in v2:
time: 57.3 us; the launch traced here: 57.2 us
  Pallas kernels  55.8 us (97%)
  local copies, waits for them, and re-layouts  1.31 us (2%)
    pallas_call x1, Pallas kernels, body(): pl.pallas_call(kernel, out_shape=jax.ShapeDtypeStruct((J * 4, TILE), BF16...  55.8 us
    unnamed x1, local copies, waits for them, and re-layouts  1.31 us

profile of v2, /device:TPU:8, one launch (start us, length us, event | category | flops | bytes accessed | tf_op | source)
XLA Modules:
  0.0 57.2 jit_solution(1462011097974118526)
XLA Ops:
  0.0 55.8 %shard_map.55 = bf16[48,128]{1,0:T(8,128)(2,1)} custom-call(s32[1,12]{1,0:T(1,128)} %pm.1, s32[1,24]{1,0:T(1,128)} %bitcast.11, bf16[12,96,128]{2,1,0:T(8,128)(2,1)} %bitcast.9, bf16[12,12,128,128]{3,2,1,0:T(8,128)(2,1)} %bitcast.7, bf16[8,384,128]{2,1,0:T(8,128)(2,1)} %bitcast.8), custom_call_target="tpu_custom_call" | custom-call | tf_op jit(solution)/shard_map/pallas_call | solution.py:250
  55.8 1.3 %copy.7 = bf16[1,12,4,128]{3,2,1,0:T(4,128)(2,1)} copy(bf16[1,12,4,128]{3,2,1,0:T(4,128)(2,1)} %bitcast.10) | data formatting | bytes 24576

commit v3 on v2

--- a/solution.py
+++ b/solution.py
@@ -13,6 +13,7 @@
 Y_FAR = (4, 3, 5, 2, 6, 1, 7)
 X_FAR = (2, 1, 3)
 GI = 16
+STEPS = 32000.0
 GC = J * GI
 GROUPS = tuple(
     tuple((dy, dx) for dy in rows for dx in (0, 1, 3, 2)) for rows in ((0, 1, 7, 2), (6, 3, 5, 4))
@@ -25,9 +26,19 @@
     return min(dy, Y - dy) + min(dx, X - dx)
 
 
+def encode(values):
+    top = jnp.max(jnp.abs(values), axis=1, keepdims=True)
+    power = jnp.ceil(jnp.log2(jnp.maximum(top, 1e-36)))
+    return jnp.round(values * jnp.exp2(-power) * STEPS).astype(jnp.int32), power
+
+
+def decode(code, power):
+    return code * (1.0 / STEPS) * jnp.exp2(power)
+
+
 def kernel(
     pm, tm, a_hbm, w_hbm, g_hbm, out,
-    av, am, wv, gv, ag, mf, rhs, pc, rc, zc, pz, rz, zr, r1, w2, w3, zz,
+    av, am, wv, gv, ag, mf, rhs, pc, rc, qc, ec, zc, pz, rz, qz, zr, r1, w2, w3, zz,
     load_sem, w_sem, ag_s, ag_r, x_s, x_r, zc_s, zc_r, zl_s, zl_r, a2a_s, a2a_r, self_sem,
 ):
     t = lax.axis_index("tensor")
@@ -39,6 +50,12 @@
 
     def column(dz):
         return {"tensor": t, "contract": lax.rem(z + dz + Z, Z) * 2 + c}
+
+    def target(k):
+        return jnp.where(k >= z, k + 1, k)
+
+    def place_of(zd):
+        return {"tensor": t, "contract": zd * 2 + c}
 
     sibling = {"tensor": t, "contract": z * 2 + 1 - c}
 
@@ -128,8 +145,13 @@
     cycle_swap.wait()
     cycle_sends = []
     rc[...] = rc[...] + pc[c]
-    for dz in Z_FAR:
-        copy = remote(rc.at[lax.rem(z + Z - dz, Z)], zc.at[dz - 1], zc_s.at[dz - 1], zc_r.at[dz - 1], column(-dz))
+    code, cycle_power = encode(rc[...])
+    qc[...] = code.astype(jnp.int16)
+    ec[...] = cycle_power
+    for k in range(Z - 1):
+        zd = target(k)
+        slot = lax.rem(z - zd + Z, Z) - 1
+        copy = remote(qc.at[zd], zc.at[slot], zc_s.at[k], zc_r.at[slot], place_of(zd))
         copy.start()
         cycle_sends.append(copy)
 
@@ -163,10 +185,14 @@
     def scatter(group):
         swaps[group].wait()
         rz[group] = rz[group] + pz[group, c]
-        for dz in Z_FAR:
+        code, power = encode(rz[group])
+        powers = [jnp.broadcast_to(p, (Z, 4, TILE)).astype(jnp.int32) for p in (power, ec[...])]
+        qz[group] = jnp.concatenate([code] + powers, axis=1).astype(jnp.int16)
+        for k in range(Z - 1):
+            zd = target(k)
+            slot = lax.rem(z - zd + Z, Z) - 1
             copy = remote(
-                rz.at[group, lax.rem(z + Z - dz, Z)], zr.at[group, dz - 1],
-                zl_s.at[group, dz - 1], zl_r.at[group, dz - 1], column(-dz),
+                qz.at[group, zd], zr.at[group, slot], zl_s.at[group, k], zl_r.at[group, slot], place_of(zd)
             )
             copy.start()
             ladder_sends.append(copy)
@@ -183,8 +209,7 @@
 
     cycle = rc[z]
     for dz in range(1, Z):
-        remote(rc.at[0], zc.at[dz - 1], zc_s.at[dz - 1], zc_r.at[dz - 1], column(-dz)).wait_recv()
-        cycle = cycle + zc[dz - 1]
+        remote(qc.at[0], zc.at[dz - 1], zc_s.at[0], zc_r.at[dz - 1], column(-dz)).wait_recv()
     for copy in cycle_sends:
         copy.wait_send()
 
@@ -194,9 +219,12 @@
         total = rz[group, z]
         for dz in (1, 11, 2, 10, 3, 9, 4, 8, 5, 7, 6):
             remote(
-                rz.at[group, 0], zr.at[group, dz - 1], zl_s.at[group, dz - 1], zl_r.at[group, dz - 1], column(-dz)
+                qz.at[group, 0], zr.at[group, dz - 1], zl_s.at[group, 0], zl_r.at[group, dz - 1], column(-dz)
             ).wait_recv()
-            total = total + zr[group, dz - 1]
+            received = zr[group, dz - 1].astype(jnp.int32).astype(F32)
+            total = total + decode(received[:24, :], received[24:25, :])
+            if group == 0:
+                cycle = cycle + decode(zc[dz - 1].astype(jnp.int32).astype(F32), received[28:29, :])
         r1[:24, :] = total
         r1[24:, :] = pltpu.roll(total[16:, :], 64, 1)
         flipped = jnp.concatenate(
@@ -262,10 +290,13 @@
             pltpu.VMEM((2, GC, CW * TILE), BF16),
             pltpu.VMEM((2, Z, J * 4, TILE), F32),
             pltpu.VMEM((Z, J * 4, TILE), F32),
-            pltpu.VMEM((Z - 1, J * 4, TILE), F32),
+            pltpu.VMEM((Z, J * 4, TILE), jnp.int16),
+            pltpu.VMEM((Z, 1, TILE), F32),
+            pltpu.VMEM((Z - 1, J * 4, TILE), jnp.int16),
             pltpu.VMEM((2, 2, Z, 24, TILE), F32),
             pltpu.VMEM((2, Z, 24, TILE), F32),
-            pltpu.VMEM((2, Z - 1, 24, TILE), F32),
+            pltpu.VMEM((2, Z, 32, TILE), jnp.int16),
+            pltpu.VMEM((2, Z - 1, 32, TILE), jnp.int16),
             pltpu.VMEM((32, TILE), F32),
             pltpu.VMEM((GI * 4, TILE), F32),
             pltpu.VMEM((2, GI, 4, TILE), F32),

time: 57.3 us -> 50.6 us (0.88)
  the two profiles are of different devices: /device:TPU:8 before, /device:TPU:1 now
where the time goes in v3:
time: 50.6 us; the launch traced here: 50.4 us
  Pallas kernels  49 us (97%)
  local copies, waits for them, and re-layouts  1.31 us (3%)
    pallas_call x1, Pallas kernels, body(): pl.pallas_call(kernel, out_shape=jax.ShapeDtypeStruct((J * 4, TILE), BF16...  49 us
    unnamed x1, local copies, waits for them, and re-layouts  1.31 us

profile of v3, /device:TPU:1, one launch (start us, length us, event | category | flops | bytes accessed | tf_op | source)
XLA Modules:
  0.0 50.4 jit_solution(6142454768451623205)
XLA Ops:
  0.0 49.0 %shard_map.55 = bf16[48,128]{1,0:T(8,128)(2,1)} custom-call(s32[1,12]{1,0:T(1,128)} %pm.1, s32[1,24]{1,0:T(1,128)} %bitcast.11, bf16[12,96,128]{2,1,0:T(8,128)(2,1)} %bitcast.9, bf16[12,12,128,128]{3,2,1,0:T(8,128)(2,1)} %bitcast.7, bf16[8,384,128]{2,1,0:T(8,128)(2,1)} %bitcast.8), custom_call_target="tpu_custom_call" | custom-call | tf_op jit(solution)/shard_map/pallas_call | solution.py:278
  49.1 1.3 %copy.7 = bf16[1,12,4,128]{3,2,1,0:T(4,128)(2,1)} copy(bf16[1,12,4,128]{3,2,1,0:T(4,128)(2,1)} %bitcast.10) | data formatting | bytes 24576

commit v4 on v3

--- a/solution.py
+++ b/solution.py
@@ -10,7 +10,7 @@
 J, WIN, TILE, CW, AB = 12, 96, 128, 8, 384
 MESH = pl.DeviceIdType.MESH
 F32, BF16 = jnp.float32, jnp.bfloat16
-Y_FAR = (4, 3, 5, 2, 6, 1, 7)
+Y_NEAR = (2, 6, 1, 7)
 X_FAR = (2, 1, 3)
 GI = 16
 STEPS = 32000.0
@@ -39,7 +39,7 @@
 def kernel(
     pm, tm, a_hbm, w_hbm, g_hbm, out,
     av, am, wv, gv, ag, mf, rhs, pc, rc, qc, ec, zc, pz, rz, qz, zr, r1, w2, w3, zz,
-    load_sem, w_sem, ag_s, ag_r, x_s, x_r, zc_s, zc_r, zl_s, zl_r, a2a_s, a2a_r, self_sem,
+    load_sem, w_sem, ag_s, ag_r, x_s, x_r, zc_s, zc_r, zl_s, zl_r, a2a_s, a2a_r, self_sem, known,
 ):
     t = lax.axis_index("tensor")
     s = lax.axis_index("contract")
@@ -66,8 +66,8 @@
 
     barrier = pltpu.get_barrier_semaphore()
     others = [(dx, dy) for dx in range(X) for dy in range(Y) if (dx, dy) != (0, 0)]
-    line = [plane(dx, dy) for dx, dy in others if 0 in (dx, dy)]
-    line += [column(dz) for dz in Z_FAR] + [sibling]
+    line = [plane(0, dy) for dy in Y_NEAR] + [plane(dx, 0) for dx in X_FAR]
+    line += [column(1), column(-1), sibling]
     for peer in line:
         pl.semaphore_signal(barrier, inc=1, device_id=peer, device_id_type=MESH)
     load_a = pltpu.make_async_copy(a_hbm, av, load_sem.at[0])
@@ -92,12 +92,21 @@
         ag[0, j * CW : (j + 1) * CW, :] = (av[j, :CW, :].astype(F32) * (m * kept)).astype(BF16)
     pl.semaphore_wait(barrier, len(line))
 
+    def tell(level):
+        for dz in (2**level, -(2**level)):
+            pl.semaphore_signal(known.at[level], inc=1, device_id=column(dz), device_id_type=MESH)
+
+    def hear(level):
+        pl.semaphore_wait(known.at[level], 2)
+
+    tell(0)
+
     def gather(dy, dx, src, to):
         slot = dy * X + dx
         return remote(src, ag.at[slot], ag_s.at[slot], ag_r.at[slot], to)
 
     gathers = []
-    for dy in Y_FAR:
+    for dy in Y_NEAR:
         gathers.append(gather(dy, 0, ag.at[0], plane(0, -dy)))
     for dx in X_FAR:
         gathers.append(gather(0, dx, ag.at[0], plane(-dx, 0)))
@@ -113,36 +122,62 @@
     for j in range(J):
         m = pm[0, j].astype(F32)
         am[:, j * TILE : (j + 1) * TILE] = (av[j].astype(F32) * m).astype(BF16)
-    left = am[...]
-    for q in range(J // 2):
+
+    def cycle_product(q):
         load_w[q].wait()
         right = jnp.concatenate(
             [wv[:, 2 * q + h].reshape(J * TILE, TILE) for h in range(2)], axis=1
         )
-        product = jnp.dot(left, right, preferred_element_type=F32)
+        product = jnp.dot(am[...], right, preferred_element_type=F32)
         for zd in range(Z):
             for cd in range(2):
                 rows = product[zd * 8 + cd * 4 : zd * 8 + cd * 4 + 4, :]
                 pc[cd, zd, 8 * q : 8 * q + 8, :] = jnp.concatenate([rows[:, :TILE], rows[:, TILE:]], axis=0)
+
+    def arrived(dy, dx):
+        gather(dy, dx, ag.at[0], sibling).wait_recv()
+
+    def pass_on(dy, dx, ey, ex):
+        copy = gather((dy + ey) % Y, (dx + ex) % X, ag.at[dy * X + dx], plane(-ex, -ey))
+        copy.start()
+        gathers.append(copy)
+
+    for q in range(3):
+        cycle_product(q)
+    arrived(2, 0)
+    pass_on(2, 0, 1, 0)
+    arrived(6, 0)
+    pass_on(6, 0, -1, 0)
+    half = jnp.where(c == 0, 2, -2)
+    copy = gather(4, 0, ag.at[jnp.where(c == 0, 2, 6) * X], plane(0, -half))
+    copy.start()
+    gathers.append(copy)
+    for dx in (1, 3, 2):
+        arrived(0, dx)
+        for ey in (2, -2) if dx == 2 else ():
+            pass_on(0, dx, ey, 0)
+        for ey in (1, -1):
+            pass_on(0, dx, ey, 0)
+    for dy in (2, 6):
+        for ex in (1, -1):
+            pass_on(dy, 0, 0, ex)
+    hear(0)
+    tell(1)
+    for q in range(3, J // 2):
+        cycle_product(q)
     cycle_swap = remote(pc.at[1 - c], rc, x_s.at[0], x_r.at[0], sibling)
     cycle_swap.start()
-
-    for dx in (1, 3, 2):
-        gather(0, dx, ag.at[0], plane(-dx, 0)).wait_recv()
-        for dy in (1, 7):
-            copy = gather(dy, dx, ag.at[dx], plane(0, -dy))
-            copy.start()
-            gathers.append(copy)
-    for dy in (2, 6, 3, 5, 4):
-        gather(dy, 0, ag.at[0], plane(0, -dy)).wait_recv()
-        for dx in X_FAR:
-            copy = gather(dy, dx, ag.at[dy * X], plane(-dx, 0))
-            copy.start()
-            gathers.append(copy)
+    for dy in (3, 5, 4):
+        arrived(dy, 0)
+        for ex in X_FAR:
+            pass_on(dy, 0, 0, ex)
+    hear(1)
+    tell(2)
     for dy in (1, 7):
-        gather(dy, 0, ag.at[0], plane(0, -dy)).wait_recv()
+        arrived(dy, 0)
 
     cycle_swap.wait()
+    hear(2)
     cycle_sends = []
     rc[...] = rc[...] + pc[c]
     code, cycle_power = encode(rc[...])
@@ -162,9 +197,8 @@
     def pick(group, ils):
         for il in ils:
             dy, dx = GROUPS[group][il]
-            if dx:
-                if dy:
-                    gather(dy, dx, ag.at[0], plane(-dx, 0)).wait_recv()
+            if dx and dy:
+                arrived(dy, dx)
             place(group, il)
 
     def multiply(group):
@@ -303,7 +337,7 @@
             pltpu.VMEM((PLANE, 4, TILE), F32),
             dma((1 + CW,)), dma((J // 2,)), dma((PLANE,)), dma((PLANE,)), dma((3,)), dma((3,)),
             dma((Z - 1,)), dma((Z - 1,)), dma((2, Z - 1)), dma((2, Z - 1)), dma((PLANE,)), dma((PLANE,)),
-            dma,
+            dma, pltpu.SemaphoreType.REGULAR((3,)),
         ],
         compiler_params=pltpu.CompilerParams(
             collective_id=0, has_side_effects=True, vmem_limit_bytes=60 * 2**20

time: 50.6 us -> 51 us (level); the launches traced: 50.4 us -> 50.1 us
  no operation moved by 1% of the time
where the time goes in v4:
time: 51 us; the launch traced here: 50.1 us
  Pallas kernels  48.8 us (96%)
  local copies, waits for them, and re-layouts  1.31 us (3%)
    pallas_call x1, Pallas kernels, body(): pl.pallas_call(kernel, out_shape=jax.ShapeDtypeStruct((J * 4, TILE), BF16...  48.8 us
    unnamed x1, local copies, waits for them, and re-layouts  1.31 us

profile of v4, /device:TPU:1, one launch (start us, length us, event | category | flops | bytes accessed | tf_op | source)
XLA Modules:
  0.0 50.1 jit_solution(6585851007520115139)
XLA Ops:
  0.0 48.8 %shard_map.55 = bf16[48,128]{1,0:T(8,128)(2,1)} custom-call(s32[1,12]{1,0:T(1,128)} %pm.1, s32[1,24]{1,0:T(1,128)} %bitcast.11, bf16[12,96,128]{2,1,0:T(8,128)(2,1)} %bitcast.9, bf16[12,12,128,128]{3,2,1,0:T(8,128)(2,1)} %bitcast.7, bf16[8,384,128]{2,1,0:T(8,128)(2,1)} %bitcast.8), custom_call_target="tpu_custom_call" | custom-call | tf_op jit(solution)/shard_map/pallas_call | solution.py:312
  48.8 1.3 %copy.7 = bf16[1,12,4,128]{3,2,1,0:T(4,128)(2,1)} copy(bf16[1,12,4,128]{3,2,1,0:T(4,128)(2,1)} %bitcast.10) | data formatting | bytes 24576

commit v5 on v4

--- a/solution.py
+++ b/solution.py
@@ -144,6 +144,8 @@
 
     for q in range(3):
         cycle_product(q)
+    hear(0)
+    tell(1)
     arrived(2, 0)
     pass_on(2, 0, 1, 0)
     arrived(6, 0)
@@ -161,8 +163,8 @@
     for dy in (2, 6):
         for ex in (1, -1):
             pass_on(dy, 0, 0, ex)
-    hear(0)
-    tell(1)
+    hear(1)
+    tell(2)
     for q in range(3, J // 2):
         cycle_product(q)
     cycle_swap = remote(pc.at[1 - c], rc, x_s.at[0], x_r.at[0], sibling)
@@ -171,8 +173,6 @@
         arrived(dy, 0)
         for ex in X_FAR:
             pass_on(dy, 0, 0, ex)
-    hear(1)
-    tell(2)
     for dy in (1, 7):
         arrived(dy, 0)
 

time: 51 us -> 48.1 us (0.943)
  Pallas kernels: 48.8 us -> 46.2 us
    pallas_call x1, Pallas kernels: 48.8 us -> 46.2 us  [body(): pl.pallas_call(kernel, out_shape=jax.ShapeDtypeStruct((J * 4, TILE), BF16...]
where the time goes in v5:
time: 48.1 us; the launch traced here: 47.5 us
  Pallas kernels  46.2 us (96%)
  local copies, waits for them, and re-layouts  1.31 us (3%)
    pallas_call x1, Pallas kernels, body(): pl.pallas_call(kernel, out_shape=jax.ShapeDtypeStruct((J * 4, TILE), BF16...  46.2 us
    unnamed x1, local copies, waits for them, and re-layouts  1.31 us

profile of v5, /device:TPU:1, one launch (start us, length us, event | category | flops | bytes accessed | tf_op | source)
XLA Modules:
  0.0 47.5 jit_solution(17149277329508053206)
XLA Ops:
  0.0 46.2 %shard_map.55 = bf16[48,128]{1,0:T(8,128)(2,1)} custom-call(s32[1,12]{1,0:T(1,128)} %pm.1, s32[1,24]{1,0:T(1,128)} %bitcast.11, bf16[12,96,128]{2,1,0:T(8,128)(2,1)} %bitcast.9, bf16[12,12,128,128]{3,2,1,0:T(8,128)(2,1)} %bitcast.7, bf16[8,384,128]{2,1,0:T(8,128)(2,1)} %bitcast.8), custom_call_target="tpu_custom_call" | custom-call | tf_op jit(solution)/shard_map/pallas_call | solution.py:312
  46.2 1.3 %copy.7 = bf16[1,12,4,128]{3,2,1,0:T(4,128)(2,1)} copy(bf16[1,12,4,128]{3,2,1,0:T(4,128)(2,1)} %bitcast.10) | data formatting | bytes 24576

commit v6 on v5

--- a/solution.py
+++ b/solution.py
@@ -12,11 +12,12 @@
 F32, BF16 = jnp.float32, jnp.bfloat16
 Y_NEAR = (2, 6, 1, 7)
 X_FAR = (2, 1, 3)
-GI = 16
+GN = 4
+GI = 8
 STEPS = 32000.0
 GC = J * GI
 GROUPS = tuple(
-    tuple((dy, dx) for dy in rows for dx in (0, 1, 3, 2)) for rows in ((0, 1, 7, 2), (6, 3, 5, 4))
+    tuple((dy, dx) for dy in rows for dx in (0, 1, 3, 2)) for rows in ((0, 1), (7, 2), (6, 3), (5, 4))
 )
 Z_FAR = (6, 5, 7, 4, 8, 3, 9, 2, 10, 1, 11)
 
@@ -26,8 +27,10 @@
     return min(dy, Y - dy) + min(dx, X - dx)
 
 
-def encode(values):
+def encode(values, shifts=()):
     top = jnp.max(jnp.abs(values), axis=1, keepdims=True)
+    for shift in shifts:
+        top = jnp.maximum(top, pltpu.roll(top, shift, 2))
     power = jnp.ceil(jnp.log2(jnp.maximum(top, 1e-36)))
     return jnp.round(values * jnp.exp2(-power) * STEPS).astype(jnp.int32), power
 
@@ -38,7 +41,7 @@
 
 def kernel(
     pm, tm, a_hbm, w_hbm, g_hbm, out,
-    av, am, wv, gv, ag, mf, rhs, pc, rc, qc, ec, zc, pz, rz, qz, zr, r1, w2, w3, zz,
+    av, am, wv, gv, ag, mf, rhs, pc, rc, qc, zc, pz, rz, qz, zr, r1, w2, w3, zz,
     load_sem, w_sem, ag_s, ag_r, x_s, x_r, zc_s, zc_r, zl_s, zl_r, a2a_s, a2a_r, self_sem, known,
 ):
     t = lax.axis_index("tensor")
@@ -180,9 +183,9 @@
     hear(2)
     cycle_sends = []
     rc[...] = rc[...] + pc[c]
-    code, cycle_power = encode(rc[...])
-    qc[...] = code.astype(jnp.int16)
-    ec[...] = cycle_power
+    code, power = encode(rc[...])
+    power = jnp.broadcast_to(power, (Z, 16, TILE)).astype(jnp.int32)
+    qc[...] = jnp.concatenate([code, power], axis=1).astype(jnp.int16)
     for k in range(Z - 1):
         zd = target(k)
         slot = lax.rem(z - zd + Z, Z) - 1
@@ -210,8 +213,7 @@
         for zd in range(Z):
             for cd in range(2):
                 rows = ladder[zd * 32 + cd * 16 : zd * 32 + cd * 16 + 16, :]
-                pz[group, cd, zd, :16, :] = rows[:, :TILE]
-                pz[group, cd, zd, 16:, :] = jnp.concatenate([rows[:8, TILE:], rows[8:, TILE:]], axis=1)
+                pz[group, cd, zd] = jnp.concatenate([rows, jnp.zeros((16, TILE - GC), F32)], axis=1)
         swap = remote(pz.at[group, 1 - c], rz.at[group], x_s.at[1 + group], x_r.at[1 + group], sibling)
         swap.start()
         swaps.append(swap)
@@ -219,9 +221,10 @@
     def scatter(group):
         swaps[group].wait()
         rz[group] = rz[group] + pz[group, c]
-        code, power = encode(rz[group])
-        powers = [jnp.broadcast_to(p, (Z, 4, TILE)).astype(jnp.int32) for p in (power, ec[...])]
-        qz[group] = jnp.concatenate([code] + powers, axis=1).astype(jnp.int16)
+        code, power = encode(rz[group], (32, 64))
+        column_of = lax.broadcasted_iota(jnp.int32, (Z, 16, TILE), 2)
+        power = jnp.broadcast_to(power, (Z, 16, TILE)).astype(jnp.int32)
+        qz[group] = jnp.where(column_of >= GC, power, code).astype(jnp.int16)
         for k in range(Z - 1):
             zd = target(k)
             slot = lax.rem(z - zd + Z, Z) - 1
@@ -231,43 +234,39 @@
             copy.start()
             ladder_sends.append(copy)
 
-    pick(0, range(GI))
-    multiply(0)
-    pick(1, range(4))
-    scatter(0)
-    pick(1, range(4, GI))
-    multiply(1)
+    for group in range(GN):
+        pick(group, range(GI))
+        if group:
+            scatter(group - 1)
+        multiply(group)
     for copy in gathers:
         copy.wait_send()
-    scatter(1)
+    scatter(GN - 1)
 
     cycle = rc[z]
     for dz in range(1, Z):
         remote(qc.at[0], zc.at[dz - 1], zc_s.at[0], zc_r.at[dz - 1], column(-dz)).wait_recv()
+        received = zc[dz - 1].astype(jnp.int32).astype(F32)
+        cycle = cycle + decode(received[: J * 4, :], received[J * 4 : J * 4 + 1, :])
     for copy in cycle_sends:
         copy.wait_send()
 
     lane = lax.broadcasted_iota(jnp.int32, (GI, TILE), 1)
+    lanes = lax.broadcasted_iota(jnp.int32, (16, TILE), 1)
     blocks = []
-    for group in range(2):
+    for group in range(GN):
         total = rz[group, z]
         for dz in (1, 11, 2, 10, 3, 9, 4, 8, 5, 7, 6):
             remote(
                 qz.at[group, 0], zr.at[group, dz - 1], zl_s.at[group, 0], zl_r.at[group, dz - 1], column(-dz)
             ).wait_recv()
             received = zr[group, dz - 1].astype(jnp.int32).astype(F32)
-            total = total + decode(received[:24, :], received[24:25, :])
-            if group == 0:
-                cycle = cycle + decode(zc[dz - 1].astype(jnp.int32).astype(F32), received[28:29, :])
-        r1[:24, :] = total
-        r1[24:, :] = pltpu.roll(total[16:, :], 64, 1)
-        flipped = jnp.concatenate(
-            [
-                jnp.transpose(jnp.concatenate([r1[pl.ds(16 * k + b, 4, stride=4), :] for b in range(4)], axis=0))
-                for k in range(2)
-            ],
-            axis=0,
-        )
+            power = jnp.where(lanes >= GC, received, 0.0)
+            power = power + pltpu.roll(power, 64, 1)
+            power = power + pltpu.roll(power, 32, 1)
+            total = total + decode(received, power)
+        r1[...] = total
+        flipped = jnp.transpose(jnp.concatenate([r1[pl.ds(b, 4, stride=4), :] for b in range(4)], axis=0))
         pieces = [jnp.zeros((GI, TILE), F32) for _ in range(4)]
         for j in range(J):
             block = jnp.concatenate(
@@ -320,23 +319,22 @@
             pltpu.VMEM((J, J, TILE, TILE), BF16),
             pltpu.VMEM((AB, CW * TILE), BF16),
             pltpu.VMEM((PLANE, J * CW, TILE), BF16),
-            pltpu.VMEM((2, CW * GC, TILE), F32),
-            pltpu.VMEM((2, GC, CW * TILE), BF16),
+            pltpu.VMEM((GN, CW * GC, TILE), F32),
+            pltpu.VMEM((GN, GC, CW * TILE), BF16),
             pltpu.VMEM((2, Z, J * 4, TILE), F32),
             pltpu.VMEM((Z, J * 4, TILE), F32),
-            pltpu.VMEM((Z, J * 4, TILE), jnp.int16),
-            pltpu.VMEM((Z, 1, TILE), F32),
-            pltpu.VMEM((Z - 1, J * 4, TILE), jnp.int16),
-            pltpu.VMEM((2, 2, Z, 24, TILE), F32),
-            pltpu.VMEM((2, Z, 24, TILE), F32),
-            pltpu.VMEM((2, Z, 32, TILE), jnp.int16),
-            pltpu.VMEM((2, Z - 1, 32, TILE), jnp.int16),
-            pltpu.VMEM((32, TILE), F32),
+            pltpu.VMEM((Z, J * 4 + 16, TILE), jnp.int16),
+            pltpu.VMEM((Z - 1, J * 4 + 16, TILE), jnp.int16),
+            pltpu.VMEM((GN, 2, Z, 16, TILE), F32),
+            pltpu.VMEM((GN, Z, 16, TILE), F32),
+            pltpu.VMEM((GN, Z, 16, TILE), jnp.int16),
+            pltpu.VMEM((GN, Z - 1, 16, TILE), jnp.int16),
+            pltpu.VMEM((16, TILE), F32),
             pltpu.VMEM((GI * 4, TILE), F32),
-            pltpu.VMEM((2, GI, 4, TILE), F32),
+            pltpu.VMEM((GN, GI, 4, TILE), F32),
             pltpu.VMEM((PLANE, 4, TILE), F32),
-            dma((1 + CW,)), dma((J // 2,)), dma((PLANE,)), dma((PLANE,)), dma((3,)), dma((3,)),
-            dma((Z - 1,)), dma((Z - 1,)), dma((2, Z - 1)), dma((2, Z - 1)), dma((PLANE,)), dma((PLANE,)),
+            dma((1 + CW,)), dma((J // 2,)), dma((PLANE,)), dma((PLANE,)), dma((1 + GN,)), dma((1 + GN,)),
+            dma((Z - 1,)), dma((Z - 1,)), dma((GN, Z - 1)), dma((GN, Z - 1)), dma((PLANE,)), dma((PLANE,)),
             dma, pltpu.SemaphoreType.REGULAR((3,)),
         ],
         compiler_params=pltpu.CompilerParams(

time: 48.1 us -> 53.9 us (1.12)
  Pallas kernels: 46.2 us -> 51.5 us
    pallas_call x1, Pallas kernels: 46.2 us -> 51.5 us  [body(): pl.pallas_call(kernel, out_shape=jax.ShapeDtypeStruct((J * 4, TILE), BF16...]
where the time goes in v6:
time: 53.9 us; the launch traced here: 52.8 us
  Pallas kernels  51.5 us (96%)
  local copies, waits for them, and re-layouts  1.31 us (2%)
    pallas_call x1, Pallas kernels, body(): pl.pallas_call(kernel, out_shape=jax.ShapeDtypeStruct((J * 4, TILE), BF16...  51.5 us
    unnamed x1, local copies, waits for them, and re-layouts  1.31 us

profile of v6, /device:TPU:1, one launch (start us, length us, event | category | flops | bytes accessed | tf_op | source)
XLA Modules:
  0.0 52.8 jit_solution(7251631348214380467)
XLA Ops:
  0.0 51.5 %shard_map.55 = bf16[48,128]{1,0:T(8,128)(2,1)} custom-call(s32[1,12]{1,0:T(1,128)} %pm.1, s32[1,24]{1,0:T(1,128)} %bitcast.11, bf16[12,96,128]{2,1,0:T(8,128)(2,1)} %bitcast.9, bf16[12,12,128,128]{3,2,1,0:T(8,128)(2,1)} %bitcast.7, bf16[8,384,128]{2,1,0:T(8,128)(2,1)} %bitcast.8), custom_call_target="tpu_custom_call" | custom-call | tf_op jit(solution)/shard_map/pallas_call | solution.py:311
  51.5 1.3 %copy.7 = bf16[1,12,4,128]{3,2,1,0:T(4,128)(2,1)} copy(bf16[1,12,4,128]{3,2,1,0:T(4,128)(2,1)} %bitcast.10) | data formatting | bytes 24576

commit v7 on v5

--- a/solution.py
+++ b/solution.py
@@ -106,10 +106,8 @@
         return remote(src, ag.at[slot], ag_s.at[slot], ag_r.at[slot], to)
 
     gathers = []
-    for dy in Y_NEAR:
-        gathers.append(gather(dy, 0, ag.at[0], plane(0, -dy)))
-    for dx in X_FAR:
-        gathers.append(gather(0, dx, ag.at[0], plane(-dx, 0)))
+    for dy, dx in ((2, 0), (6, 0), (0, 2), (0, 1), (0, 3), (1, 0), (7, 0)):
+        gathers.append(gather(dy, dx, ag.at[0], plane(-dx, -dy)))
     for copy in gathers:
         copy.start()
 
@@ -154,15 +152,15 @@
     copy = gather(4, 0, ag.at[jnp.where(c == 0, 2, 6) * X], plane(0, -half))
     copy.start()
     gathers.append(copy)
+    for dy in (2, 6):
+        for ex in (1, -1):
+            pass_on(dy, 0, 0, ex)
     for dx in (1, 3, 2):
         arrived(0, dx)
         for ey in (2, -2) if dx == 2 else ():
             pass_on(0, dx, ey, 0)
         for ey in (1, -1):
             pass_on(0, dx, ey, 0)
-    for dy in (2, 6):
-        for ex in (1, -1):
-            pass_on(dy, 0, 0, ex)
     hear(1)
     tell(2)
     for q in range(3, J // 2):

time: 48.1 us -> 48.1 us (level)
  no operation moved by 1% of the time
where the time goes in v7:
time: 48.1 us; the launch traced here: 47.5 us
  Pallas kernels  46.2 us (96%)
  local copies, waits for them, and re-layouts  1.31 us (3%)
    pallas_call x1, Pallas kernels, body(): pl.pallas_call(kernel, out_shape=jax.ShapeDtypeStruct((J * 4, TILE), BF16...  46.2 us
    unnamed x1, local copies, waits for them, and re-layouts  1.31 us

profile of v7, /device:TPU:1, one launch (start us, length us, event | category | flops | bytes accessed | tf_op | source)
XLA Modules:
  0.0 47.5 jit_solution(8626826235268632112)
XLA Ops:
  0.0 46.2 %shard_map.55 = bf16[48,128]{1,0:T(8,128)(2,1)} custom-call(s32[1,12]{1,0:T(1,128)} %pm.1, s32[1,24]{1,0:T(1,128)} %bitcast.11, bf16[12,96,128]{2,1,0:T(8,128)(2,1)} %bitcast.9, bf16[12,12,128,128]{3,2,1,0:T(8,128)(2,1)} %bitcast.7, bf16[8,384,128]{2,1,0:T(8,128)(2,1)} %bitcast.8), custom_call_target="tpu_custom_call" | custom-call | tf_op jit(solution)/shard_map/pallas_call | solution.py:310
  46.2 1.3 %copy.7 = bf16[1,12,4,128]{3,2,1,0:T(4,128)(2,1)} copy(bf16[1,12,4,128]{3,2,1,0:T(4,128)(2,1)} %bitcast.10) | data formatting | bytes 24576
